TPU v7x, 256 devices: a whole 4x4x8 slice. The times are simulated.
256 devices in a mesh: expert: 64 (over x, z, core), fsdp: 4 (over y).
Axes of the slice: x: 4, y: 4, z: 8, core: 2. Of those that a mesh axis runs over, the one named last changes fastest.
Arguments:
- teacher_in: bfloat16 [8192, 4096], P('expert'), may hold values from -6 to 6
- routes: int32 [8192, 8], P('expert'), may hold values from 0 to 63, all different within a row; in each aligned block of 128 rows (0 to 127, 128 to 255, ...) at most 18 rows name the same one
- route_weights: float32 [8192, 8], P('expert'), may hold values from 0.1 to 0.5
- expert_gate_up: bfloat16 [64, 4096, 2, 1024], P('expert', None, None, 'fsdp'), may hold values from -0.09375 to 0.09375
- expert_down: bfloat16 [64, 1024, 4096], P('expert', 'fsdp'), may hold values from -0.1875 to 0.1875
- student_in: bfloat16 [8192, 2048], P('expert'), may hold values from -16 to 16
- norm_gain: float32 [2048], replicated, may hold values from 0.5 to 2
- projector: bfloat16 [2048, 4096], P(None, 'fsdp'), may hold values from -0.125 to 0.125
- second_moment: float32 [2048, 4096], P('expert', 'fsdp'), may hold values from 2048 to 32768
Outputs:
- d_student: bfloat16 [8192, 2048], P('expert')
- proj_step: float32 [2048, 4096], P('expert', 'fsdp')
Inputs may be any that keep to these rules, and one draw needn't show every extreme that they name: `routes`: each row names 8 different experts; in each block of 128 consecutive rows (the rows of one index of expert) no expert is named by more than 18 rows.
All inputs are finite; a program needn't handle non-finite values.
Results may differ from a plain program's by a relative error of at most 0.02.
Values may be sent and summed in bfloat16 or wider, within the bound.
A program may use at most 128 MiB of HBM per device.

v0:
```python
import jax
import jax.numpy as jnp
from jax import lax
from jax.sharding import PartitionSpec as P

beta_two = 0.95


def slot_maps(routes, route_weights, experts):
    tokens = routes.shape[0]
    named = routes[:, :, None] == jnp.arange(experts, dtype=jnp.int32)[None, None, :]
    member = jnp.any(named, axis=1)
    weight = jnp.sum(jnp.where(named, route_weights[:, :, None], 0.0), axis=1)
    earlier = jnp.tril(jnp.ones((tokens, tokens), jnp.bfloat16), -1)
    before = jnp.dot(earlier, member.astype(jnp.bfloat16), preferred_element_type=jnp.float32)
    position = jnp.where(member, before.astype(jnp.int32), -1)
    return (position.T, weight.T)


def per_device(
    teacher_in,
    routes,
    route_weights,
    expert_gate_up,
    expert_down,
    student_in,
    norm_gain,
    projector,
    second_moment,
):
    tokens_here, model_width = teacher_in.shape
    top_count = routes.shape[1]
    experts = lax.axis_size("expert")
    shares = lax.axis_size("fsdp")
    part = model_width // shares
    capacity = min(tokens_here, tokens_here * top_count * 9 // (8 * experts))
    position, weight = slot_maps(routes, route_weights, experts)
    onehot = position[:, None, :] == jnp.arange(capacity, dtype=jnp.int32)[None, :, None]
    select = onehot.astype(jnp.bfloat16)
    weighted = jnp.where(onehot, weight[:, None, :], 0.0)
    high = weighted.astype(jnp.bfloat16)
    low = (weighted - high.astype(jnp.float32)).astype(jnp.bfloat16)
    mine = lax.axis_index("fsdp") * part
    columns = lax.dynamic_slice_in_dim(teacher_in, mine, part, axis=1)
    buffer = jnp.einsum("est,tc->esc", select, columns, preferred_element_type=jnp.float32)
    buffer = buffer.astype(jnp.bfloat16)
    received = lax.all_to_all(buffer, "expert", split_axis=0, concat_axis=0, tiled=True)
    rows = lax.all_gather(received, "fsdp", axis=0)
    down_rows = lax.all_to_all(expert_down[0], "fsdp", split_axis=1, concat_axis=0, tiled=True)
    gate_up = expert_gate_up.reshape(shares, part, -1)
    gate_up_out = jnp.einsum("yesc,ycn->esn", rows, gate_up, preferred_element_type=jnp.float32)
    half = gate_up_out.shape[2] // 2
    hidden = (jax.nn.silu(gate_up_out[:, :, :half]) * gate_up_out[:, :, half:]).astype(jnp.bfloat16)
    hidden_all = lax.all_gather(hidden, "fsdp", axis=0)
    expert_out = jnp.einsum(
        "yesh,yhc->esc",
        hidden_all,
        down_rows.reshape(shares, half, part),
        preferred_element_type=jnp.float32,
    )
    returned = lax.all_to_all(
        expert_out.astype(jnp.bfloat16), "expert", split_axis=0, concat_axis=0, tiled=True
    )
    teacher = jnp.einsum(
        "est,esc->tc", high, returned, preferred_element_type=jnp.float32
    ) + jnp.einsum("est,esc->tc", low, returned, preferred_element_type=jnp.float32)
    student_wide = student_in.astype(jnp.float32)
    inv_rms = lax.rsqrt(jnp.mean(student_wide * student_wide, axis=1, keepdims=True) + 1e-06)
    normed = student_wide * inv_rms
    student_feat = (normed * norm_gain[None, :]).astype(jnp.bfloat16)
    residue = (
        jnp.dot(student_feat, projector, preferred_element_type=jnp.float32) - teacher
    ).astype(jnp.bfloat16)
    feat_part = jnp.einsum("tc,dc->td", residue, projector, preferred_element_type=jnp.float32)
    feat_grad = lax.psum(feat_part.astype(jnp.bfloat16), "fsdp").astype(jnp.float32)
    scaled = feat_grad * norm_gain[None, :]
    d_student = (
        inv_rms * (scaled - normed * jnp.mean(scaled * normed, axis=1, keepdims=True))
    ).astype(jnp.bfloat16)
    grad_block = lax.psum_scatter(
        jnp.einsum("tr,tc->rc", student_feat, residue, preferred_element_type=jnp.float32),
        "expert",
        scatter_dimension=0,
        tiled=True,
    )
    proj_step = grad_block / jnp.sqrt(
        beta_two * second_moment + (1.0 - beta_two) * grad_block * grad_block
    )
    return (d_student, proj_step)


def solution(mesh):
    placed = (
        P("expert", None),
        P("expert", None),
        P("expert", None),
        P("expert", None, None, "fsdp"),
        P("expert", "fsdp", None),
        P("expert", None),
        P(),
        P(None, "fsdp"),
        P("expert", "fsdp"),
    )
    return jax.shard_map(
        per_device,
        mesh=mesh,
        in_specs=placed,
        out_specs=(P("expert", None), P("expert", "fsdp")),
        check_vma=False,
    )
```

profile of v0, /device:TPU:8, one launch (start us, length us, event | category | flops | bytes accessed | tf_op | source)
XLA Modules:
  0.0 567.9 jit_solution(15985997728687819142)
XLA Ops:
  7.2 0.0 copy-start
  7.2 0.0 all-gather.5.cloned.1.call-start
  7.2 0.8 fusion.37
  8.0 0.2 fusion.19
  8.3 0.2 copy-done
  8.4 0.8 convolution_convert_fusion.1
  9.2 1.4 copy.35
  10.6 84.8 %all_to_all.26 = bf16[64,18,1024]{2,1,0:T(8,128)(2,1)S(1)} all-to-all(bf16[64,18,1024]{2,1,0:T(8,128)(2,1)S(1)} %copy.35), channel_id=1, replica_groups=mesh['expert'=64,'fsdp'=4] {'expert'}, dimensions={0} | all-to-all | bytes 4718592 | tf_op jit(solution)/shard_map/all_to_all | solution.py:47
  95.4 2.7 copy.36
  98.1 0.0 all-gather.5.cloned.1.call-update
  98.1 0.0 all-gather.7.cloned.1.call-start
  98.1 7.6 %reshape.34 = bf16[4,1024,512,1]{2,1,0,3:T(8,128)(2,1)} reshape(bf16[1,4096,2,256]{3,2,1,0:T(2,128)(2,1)} %param.12) | data formatting | bytes 8388608 | tf_op jit(solution)/shard_map/reshape | solution.py:50
  105.7 84.6 %all-gather.5.cloned.1.call-done = bf16[256,18,1024]{2,0,1:T(8,128)(2,1)} async-done(((bf16[64,18,1024]{2,0,1:T(8,128)(2,1)}), bf16[256,18,1024]{2,0,1:T(8,128)(2,1)}) %all-gather.5.cloned.1.call-update) | async-done | bytes 9437200 | tf_op jit(solution)/shard_map/all_gather | solution.py:48
  190.3 8.8 %convolution_bitcast_fusion = f32[64,18,512]{2,0,1:T(8,128)S(1)} fusion(bf16[4,64,18,1024]{3,1,0,2:T(8,128)(2,1)} %bitcast.37, bf16[4,1024,512,1]{2,1,0,3:T(8,128)(2,1)} %reshape.34), kind=kOutput, calls=%fused_computation.4 | convolution fusion | flops 4831838208 | bytes 15990784 | tf_op jit(solution)/shard_map/yesc,ycn->esn/dot_general | solution.py:51
  199.2 0.0 copy-start.4
  199.2 1.2 fusion.18
  200.4 0.0 all-gather.7.cloned.1.call-update
  200.4 0.6 copy-done.4
  201.0 2.4 copy.37
  203.4 3.0 copy.38
  206.4 48.3 %all_to_all.27 = bf16[256,4,1024]{2,0,1:T(8,128)(2,1)} all-to-all(bf16[256,4,1024]{2,0,1:T(8,128)(2,1)S(1)} %copy.38), channel_id=1, replica_groups=mesh['expert'=64,'fsdp'=4] {'fsdp'}, dimensions={1} | all-to-all | bytes 4194304 | tf_op jit(solution)/shard_map/all_to_all | solution.py:49
  254.7 0.0 all-gather.7.cloned.1.call-done
  254.7 4.9 bitcast_convert_fusion
  259.6 3.1 copy.39
  262.7 0.0 copy-start.7
  262.7 0.0 copy-start.8
  262.7 0.0 copy-start.3
  262.7 10.8 %all-to-all-start.2 = ((bf16[64,18,1024]{2,1,0:T(8,128)(2,1)}), bf16[64,18,1024]{2,1,0:T(8,128)(2,1)}, u32[]{:S(2)}, u32[]{:S(2)}) async-start(bf16[64,18,1024]{2,1,0:T(8,128)(2,1)} %copy.39), calls=%async_computation.2 | async-start | bytes 6291456 | tf_op jit(solution)/shard_map/all_to_all | solution.py:61
  273.5 0.0 all-reduce.2.cloned.1.call-start
  273.5 0.0 copy-done.7
  273.5 0.0 copy-done.8
  273.6 0.0 copy-done.3
  273.6 0.2 fusion.25
  273.8 72.9 %all-to-all-done.2 = bf16[64,18,1024]{2,1,0:T(8,128)(2,1)} async-done(((bf16[64,18,1024]{2,1,0:T(8,128)(2,1)}), bf16[64,18,1024]{2,1,0:T(8,128)(2,1)}, u32[]{:S(2)}, u32[]{:S(2)}) %all-to-all-start.2) | async-done | bytes 2359328 | tf_op jit(solution)/shard_map/all_to_all | solution.py:61
  346.7 0.0 copy-start.2
  346.7 4.8 fusion.8
  351.5 0.0 copy-start.5
  351.5 4.7 fusion.14
  356.2 0.0 copy-done.2
  356.2 0.0 copy-done.5
  356.2 0.8 fusion.17
  357.1 2.3 convolution_convert_fusion
  359.4 0.0 all-reduce.2.cloned.1.call-update
  359.4 0.0 reduce-scatter.2.cloned.1.call-start
  359.4 4.6 fusion.38
  364.0 0.0 reduce-scatter.2.cloned.1.call-update
  364.1 0.0 copy-start.6
  364.1 0.0 copy-start.1
  364.1 38.8 %all-reduce.2.cloned.1.call-done = bf16[128,2048]{1,0:T(8,128)(2,1)} async-done(((bf16[128,2048]{1,0:T(8,128)(2,1)}), bf16[128,2048]{1,0:T(8,128)(2,1)}) %all-reduce.2.cloned.1.call-update) | async-done | bytes 524304 | tf_op jit(solution)/shard_map/psum | solution.py:75
  402.9 1.4 fusion.21
  404.3 2.2 fusion.24
  406.5 153.3 %reduce-scatter.2.cloned.1.call-done = f32[32,1024]{1,0:T(8,128)} async-done(((f32[2048,1024]{1,0:T(8,128)}), f32[32,1024]{1,0:T(8,128)}) %reduce-scatter.2.cloned.1.call-update) | async-done | bytes 131088 | tf_op jit(solution)/shard_map/reduce_scatter | solution.py:80
  559.8 0.0 copy-done.6
  559.8 1.6 fusion.43
  561.4 0.0 copy-done.1
  (4 shorter events, 0.1 us)
Async XLA Ops:
  7.2 1.2 copy-start
  7.2 183.2 %all-gather.5.cloned.1.call-start = ((), (), s32[]{:S(2)}) async-start(), calls=%async_computation.6 | async-start | bytes 11796480 | tf_op jit(solution)/shard_map/all_gather | solution.py:48
  98.1 156.6 %all-gather.7.cloned.1.call-start = ((), (), s32[]{:S(2)}) async-start(), calls=%async_computation.7 | async-start | bytes 2949120 | tf_op jit(solution)/shard_map/all_gather | solution.py:54
  199.2 1.8 copy-start.4
  262.7 10.9 %copy-start.7 = (s32[128,8]{0,1:T(8,128)S(1)}, s32[128,8]{0,1:T(8,128)}, u32[]{:S(2)}) copy-start(s32[128,8]{0,1:T(8,128)} %param.10) | copy-start | bytes 12292
  262.7 10.9 %copy-start.8 = (f32[128,8]{0,1:T(8,128)S(1)}, f32[128,8]{0,1:T(8,128)}, u32[]{:S(2)}) copy-start(f32[128,8]{0,1:T(8,128)} %param.11) | copy-start | bytes 12292
  262.7 10.9 %copy-start.3 = (bf16[128,2048]{1,0:T(8,128)(2,1)S(1)}, bf16[128,2048]{1,0:T(8,128)(2,1)}, u32[]{:S(2)}) copy-start(bf16[128,2048]{1,0:T(8,128)(2,1)} %param.14) | copy-start | bytes 1572868
  262.7 84.0 %all-to-all-start.2 = ((bf16[64,18,1024]{2,1,0:T(8,128)(2,1)}), bf16[64,18,1024]{2,1,0:T(8,128)(2,1)}, u32[]{:S(2)}, u32[]{:S(2)}) async-start(bf16[64,18,1024]{2,1,0:T(8,128)(2,1)} %copy.39), calls=%async_computation.2 | async-start | bytes 6291456 | tf_op jit(solution)/shard_map/all_to_all | solution.py:61
  273.5 129.4 %all-reduce.2.cloned.1.call-start = ((), (), s32[]{:S(2)}) async-start(), calls=%async_computation.4 | async-start | bytes 1048576 | tf_op jit(solution)/shard_map/psum | solution.py:75
  346.7 9.5 %copy-start.2 = (bf16[2048,1024]{1,0:T(8,128)(2,1)S(1)}, bf16[2048,1024]{1,0:T(8,128)(2,1)}, u32[]{:S(2)}) copy-start(bf16[2048,1024]{1,0:T(8,128)(2,1)} %param.16) | copy-start | bytes 12582916
  351.5 4.7 copy-start.5
  359.4 200.4 %reduce-scatter.2.cloned.1.call-start = ((), (), s32[]{:S(2)}) async-start(), calls=%async_computation.5 | async-start | bytes 8519680 | tf_op jit(solution)/shard_map/reduce_scatter | solution.py:80
  364.1 195.8 %copy-start.6 = (f32[32,1024]{1,0:T(8,128)S(1)}, f32[32,1024]{1,0:T(8,128)}, u32[]{:S(2)}) copy-start(f32[32,1024]{1,0:T(8,128)} %param.17) | copy-start | bytes 393220
  364.1 197.3 %copy-start.1 = (bf16[128,4096]{1,0:T(8,128)(2,1)S(1)}, bf16[128,4096]{1,0:T(8,128)(2,1)}, u32[]{:S(2)}) copy-start(bf16[128,4096]{1,0:T(8,128)(2,1)} %param.9) | copy-start | bytes 3145732
Sparse Core Ops, SparseCore 0:
  98.2 92.1 all-gather.4
  200.5 53.4 all-gather.6
  359.5 43.3 all-reduce.1
  407.0 152.7 reduce-scatter.1
where the time goes:
time: 569 us; the launch traced here: 568 us
  waiting for transfers between devices  350 us (62%)
  blocking collectives  133 us (23%)
  matrix products  31.9 us (6%)
  local copies, waits for them, and re-layouts  20.9 us (4%)
  between operations  13.9 us (2%)
  starting transfers between devices  11 us (2%)
  other arithmetic  7.36 us (1%)
    reduce_scatter x1, waiting for transfers between devices, per_device(): lax.psum_scatter(jnp.einsum('tr,tc->rc', student_feat, residue, preferred...  153 us
    all_to_all x1, blocking collectives, per_device(): lax.all_to_all(buffer, 'expert', split_axis=0, concat_axis=0, tiled=True)  84.8 us
    all_gather x1, waiting for transfers between devices, per_device(): rows = lax.all_gather(received, 'fsdp', axis=0)  84.6 us
    all_to_all x1, waiting for transfers between devices, per_device(): lax.all_to_all(expert_out.astype(jnp.bfloat16), 'expert', split_axis=0, c...  72.9 us
    all_to_all x1, blocking collectives, per_device(): lax.all_to_all(expert_down[0], 'fsdp', split_axis=1, concat_axis=0, tiled...  48.3 us
    psum x1, waiting for transfers between devices, per_device(): lax.psum(feat_part.astype(jnp.bfloat16), 'fsdp').astype(jnp.float32)  38.8 us
  transfers between devices with their start and end apart: 5, of which 4 were waited for; matrix products, arithmetic and copies ran while one was open for 4% of the time, Pallas kernels for 0%

commit v1 on v0

--- a/solution.py
+++ b/solution.py
@@ -72,7 +72,9 @@
         jnp.dot(student_feat, projector, preferred_element_type=jnp.float32) - teacher
     ).astype(jnp.bfloat16)
     feat_part = jnp.einsum("tc,dc->td", residue, projector, preferred_element_type=jnp.float32)
-    feat_grad = lax.psum(feat_part.astype(jnp.bfloat16), "fsdp").astype(jnp.float32)
+    feat_grad = jnp.sum(lax.all_gather(feat_part.astype(jnp.bfloat16), "fsdp"), axis=0).astype(
+        jnp.float32
+    )
     scaled = feat_grad * norm_gain[None, :]
     d_student = (
         inv_rms * (scaled - normed * jnp.mean(scaled * normed, axis=1, keepdims=True))

time: 569 us -> 554 us (0.974)
  waiting for transfers between devices: 350 us -> 335 us
    psum x1 -> x0, waiting for transfers between devices: 38.8 us -> none  [per_device(): lax.psum(feat_part.astype(jnp.bfloat16), 'fsdp').astype(jnp.float32)]
    all_gather x0 -> x1, waiting for transfers between devices: none -> 24.2 us  [per_device(): lax.all_gather(feat_part.astype(jnp.bfloat16), 'fsdp')]
where the time goes in v1:
time: 554 us; the launch traced here: 553 us
  waiting for transfers between devices  335 us (60%)
  blocking collectives  133 us (24%)
  matrix products  31.9 us (6%)
  local copies, waits for them, and re-layouts  20.9 us (4%)
  between operations  13.9 us (3%)
  starting transfers between devices  11 us (2%)
  other arithmetic  7.4 us (1%)
    reduce_scatter x1, waiting for transfers between devices, per_device(): lax.psum_scatter(jnp.einsum('tr,tc->rc', student_feat, residue, preferred...  153 us
    all_to_all x1, blocking collectives, per_device(): lax.all_to_all(buffer, 'expert', split_axis=0, concat_axis=0, tiled=True)  84.8 us
    all_gather x1, waiting for transfers between devices, per_device(): rows = lax.all_gather(received, 'fsdp', axis=0)  84.6 us
    all_to_all x1, waiting for transfers between devices, per_device(): lax.all_to_all(expert_out.astype(jnp.bfloat16), 'expert', split_axis=0, c...  72.9 us
    all_to_all x1, blocking collectives, per_device(): lax.all_to_all(expert_down[0], 'fsdp', split_axis=1, concat_axis=0, tiled...  48.3 us
    all_gather x1, waiting for transfers between devices, per_device(): lax.all_gather(feat_part.astype(jnp.bfloat16), 'fsdp')  24.2 us
  transfers between devices with their start and end apart: 5, of which 4 were waited for; matrix products, arithmetic and copies ran while one was open for 4% of the time, Pallas kernels for 0%

profile of v1, /device:TPU:8, one launch (start us, length us, event | category | flops | bytes accessed | tf_op | source)
XLA Modules:
  0.0 553.0 jit_solution(15871186206869330192)
XLA Ops:
  7.2 0.0 copy-start
  7.2 0.0 all-gather.7.cloned.1.call-start
  7.2 0.8 fusion.37
  8.0 0.2 fusion.19
  8.3 0.2 copy-done
  8.4 0.8 convolution_convert_fusion.1
  9.2 1.4 copy.35
  10.6 84.8 %all_to_all.26 = bf16[64,18,1024]{2,1,0:T(8,128)(2,1)S(1)} all-to-all(bf16[64,18,1024]{2,1,0:T(8,128)(2,1)S(1)} %copy.35), channel_id=1, replica_groups=mesh['expert'=64,'fsdp'=4] {'expert'}, dimensions={0} | all-to-all | bytes 4718592 | tf_op jit(solution)/shard_map/all_to_all | solution.py:47
  95.4 2.7 copy.36
  98.1 0.0 all-gather.7.cloned.1.call-update
  98.1 0.0 all-gather.9.cloned.1.call-start
  98.1 7.6 %reshape.35 = bf16[4,1024,512,1]{2,1,0,3:T(8,128)(2,1)} reshape(bf16[1,4096,2,256]{3,2,1,0:T(2,128)(2,1)} %param.12) | data formatting | bytes 8388608 | tf_op jit(solution)/shard_map/reshape | solution.py:50
  105.7 84.6 %all-gather.7.cloned.1.call-done = bf16[256,18,1024]{2,0,1:T(8,128)(2,1)} async-done(((bf16[64,18,1024]{2,0,1:T(8,128)(2,1)}), bf16[256,18,1024]{2,0,1:T(8,128)(2,1)}) %all-gather.7.cloned.1.call-update) | async-done | bytes 9437200 | tf_op jit(solution)/shard_map/all_gather | solution.py:48
  190.3 8.8 %convolution_bitcast_fusion = f32[64,18,512]{2,0,1:T(8,128)S(1)} fusion(bf16[4,64,18,1024]{3,1,0,2:T(8,128)(2,1)} %bitcast.39, bf16[4,1024,512,1]{2,1,0,3:T(8,128)(2,1)} %reshape.35), kind=kOutput, calls=%fused_computation.4 | convolution fusion | flops 4831838208 | bytes 15990784 | tf_op jit(solution)/shard_map/yesc,ycn->esn/dot_general | solution.py:51
  199.2 0.0 copy-start.4
  199.2 1.2 fusion.18
  200.4 0.0 all-gather.9.cloned.1.call-update
  200.4 0.6 copy-done.4
  201.0 2.4 copy.37
  203.4 3.0 copy.38
  206.4 48.3 %all_to_all.27 = bf16[256,4,1024]{2,0,1:T(8,128)(2,1)} all-to-all(bf16[256,4,1024]{2,0,1:T(8,128)(2,1)S(1)} %copy.38), channel_id=1, replica_groups=mesh['expert'=64,'fsdp'=4] {'fsdp'}, dimensions={1} | all-to-all | bytes 4194304 | tf_op jit(solution)/shard_map/all_to_all | solution.py:49
  254.7 0.0 all-gather.9.cloned.1.call-done
  254.7 4.9 bitcast_convert_fusion
  259.6 3.1 copy.39
  262.7 0.0 copy-start.7
  262.7 0.0 copy-start.8
  262.7 0.0 copy-start.3
  262.7 10.8 %all-to-all-start.2 = ((bf16[64,18,1024]{2,1,0:T(8,128)(2,1)}), bf16[64,18,1024]{2,1,0:T(8,128)(2,1)}, u32[]{:S(2)}, u32[]{:S(2)}) async-start(bf16[64,18,1024]{2,1,0:T(8,128)(2,1)} %copy.39), calls=%async_computation.2 | async-start | bytes 6291456 | tf_op jit(solution)/shard_map/all_to_all | solution.py:61
  273.5 0.0 all-gather.11.cloned.1.call-start
  273.5 0.0 copy-done.7
  273.5 0.0 copy-done.8
  273.6 0.0 copy-done.3
  273.6 0.2 fusion.25
  273.8 72.9 %all-to-all-done.2 = bf16[64,18,1024]{2,1,0:T(8,128)(2,1)} async-done(((bf16[64,18,1024]{2,1,0:T(8,128)(2,1)}), bf16[64,18,1024]{2,1,0:T(8,128)(2,1)}, u32[]{:S(2)}, u32[]{:S(2)}) %all-to-all-start.2) | async-done | bytes 2359328 | tf_op jit(solution)/shard_map/all_to_all | solution.py:61
  346.7 0.0 copy-start.2
  346.7 4.8 fusion.8
  351.5 0.0 copy-start.5
  351.5 4.7 fusion.14
  356.2 0.0 copy-done.2
  356.2 0.0 copy-done.5
  356.2 0.8 fusion.17
  357.1 2.3 convolution_convert_fusion
  359.4 0.0 all-gather.11.cloned.1.call-update
  359.4 0.0 reduce-scatter.2.cloned.1.call-start
  359.4 4.6 fusion.38
  364.0 0.0 reduce-scatter.2.cloned.1.call-update
  364.1 24.2 %all-gather.11.cloned.1.call-done = bf16[512,2048]{1,0:T(8,128)(2,1)} async-done(((bf16[128,2048]{1,0:T(8,128)(2,1)}), bf16[512,2048]{1,0:T(8,128)(2,1)}) %all-gather.11.cloned.1.call-update) | async-done | bytes 2097168 | tf_op jit(solution)/shard_map/all_gather | solution.py:75
  388.2 0.0 copy-start.1
  388.2 0.0 copy-start.6
  388.2 2.1 reduce_sum.41
  390.3 0.3 fusion.21
  390.7 1.2 fusion.24
  391.8 153.1 %reduce-scatter.2.cloned.1.call-done = f32[32,1024]{1,0:T(8,128)} async-done(((f32[2048,1024]{1,0:T(8,128)}), f32[32,1024]{1,0:T(8,128)}) %reduce-scatter.2.cloned.1.call-update) | async-done | bytes 131088 | tf_op jit(solution)/shard_map/reduce_scatter | solution.py:82
  544.9 0.0 copy-done.6
  544.9 1.6 fusion.43
  546.5 0.0 copy-done.1
  (4 shorter events, 0.1 us)
Async XLA Ops:
  7.2 1.2 copy-start
  7.2 183.2 %all-gather.7.cloned.1.call-start = ((), (), s32[]{:S(2)}) async-start(), calls=%async_computation.5 | async-start | bytes 11796480 | tf_op jit(solution)/shard_map/all_gather | solution.py:48
  98.1 156.6 %all-gather.9.cloned.1.call-start = ((), (), s32[]{:S(2)}) async-start(), calls=%async_computation.6 | async-start | bytes 2949120 | tf_op jit(solution)/shard_map/all_gather | solution.py:54
  199.2 1.8 copy-start.4
  262.7 10.9 %copy-start.7 = (s32[128,8]{0,1:T(8,128)S(1)}, s32[128,8]{0,1:T(8,128)}, u32[]{:S(2)}) copy-start(s32[128,8]{0,1:T(8,128)} %param.10) | copy-start | bytes 12292
  262.7 10.9 %copy-start.8 = (f32[128,8]{0,1:T(8,128)S(1)}, f32[128,8]{0,1:T(8,128)}, u32[]{:S(2)}) copy-start(f32[128,8]{0,1:T(8,128)} %param.11) | copy-start | bytes 12292
  262.7 10.9 %copy-start.3 = (bf16[128,2048]{1,0:T(8,128)(2,1)S(1)}, bf16[128,2048]{1,0:T(8,128)(2,1)}, u32[]{:S(2)}) copy-start(bf16[128,2048]{1,0:T(8,128)(2,1)} %param.14) | copy-start | bytes 1572868
  262.7 84.0 %all-to-all-start.2 = ((bf16[64,18,1024]{2,1,0:T(8,128)(2,1)}), bf16[64,18,1024]{2,1,0:T(8,128)(2,1)}, u32[]{:S(2)}, u32[]{:S(2)}) async-start(bf16[64,18,1024]{2,1,0:T(8,128)(2,1)} %copy.39), calls=%async_computation.2 | async-start | bytes 6291456 | tf_op jit(solution)/shard_map/all_to_all | solution.py:61
  273.5 114.7 %all-gather.11.cloned.1.call-start = ((), (), s32[]{:S(2)}) async-start(), calls=%async_computation.7 | async-start | bytes 2621440 | tf_op jit(solution)/shard_map/all_gather | solution.py:75
  346.7 9.5 %copy-start.2 = (bf16[2048,1024]{1,0:T(8,128)(2,1)S(1)}, bf16[2048,1024]{1,0:T(8,128)(2,1)}, u32[]{:S(2)}) copy-start(bf16[2048,1024]{1,0:T(8,128)(2,1)} %param.16) | copy-start | bytes 12582916
  351.5 4.7 copy-start.5
  359.4 185.5 %reduce-scatter.2.cloned.1.call-start = ((), (), s32[]{:S(2)}) async-start(), calls=%async_computation.4 | async-start | bytes 8519680 | tf_op jit(solution)/shard_map/reduce_scatter | solution.py:82
  388.2 158.3 %copy-start.1 = (bf16[128,4096]{1,0:T(8,128)(2,1)S(1)}, bf16[128,4096]{1,0:T(8,128)(2,1)}, u32[]{:S(2)}) copy-start(bf16[128,4096]{1,0:T(8,128)(2,1)} %param.9) | copy-start | bytes 3145732
  388.2 156.7 %copy-start.6 = (f32[32,1024]{1,0:T(8,128)S(1)}, f32[32,1024]{1,0:T(8,128)}, u32[]{:S(2)}) copy-start(f32[32,1024]{1,0:T(8,128)} %param.17) | copy-start | bytes 393220
Sparse Core Ops, SparseCore 0:
  98.2 92.1 all-gather.6
  200.5 53.4 all-gather.8
  359.5 28.6 all-gather.10
  392.3 152.5 reduce-scatter.1
